TPU v7x, 32 devices: a whole 2x2x4 slice. The times are simulated.
32 devices in a mesh: groups: 2 (over y), depth: 4 (over z), rays: 4 (over x, core).
Axes of the slice: x: 2, y: 2, z: 4, core: 2. Of those that a mesh axis runs over, the one named last changes fastest.
Arguments:
- brick_features: bfloat16 [16, 8, 4, 16384], P(None, ('groups', 'depth'), 'rays'), parts along dimension 1, may hold values from -6 to 6
- entry_cells: int32 [8, 4, 1024], P(('groups', 'depth'), 'rays'), parts along dimension 0, may hold values from 0 to 16368
- sample_counts: int32 [8, 4, 1024], P(('groups', 'depth'), 'rays'), parts along dimension 0, may hold values from 1 to 16, as said below
- brick_rank: int32 [8, 4], P(('groups', 'rays')), parts along dimension 0, may hold values from 0 to 3, each once within a row
- input_layer_weight: bfloat16 [16, 128], replicated, may hold values from -1.5 to 1.5
- second_weight: bfloat16 [128, 33], replicated, may hold values from -0.5 to 0.5
- conv_in: bfloat16 [9, 32, 128], replicated, may hold values from -0.375 to 0.375
- conv_mid: bfloat16 [9, 128, 128], replicated, may hold values from -0.1875 to 0.1875
- conv_out: bfloat16 [9, 128, 128], replicated, may hold values from -0.1875 to 0.1875
Outputs:
- frame: bfloat16 [128, 64, 128], P(('groups', 'depth'), 'rays'), parts along dimension 0
There are 2 independent parts, one for each index of `groups`. A program takes and returns all parts, laid end to end along the dimension named above; an argument that names none is the same for every part. Nothing has to cross between parts.
Inputs may be any that keep to these rules, and one draw needn't show every extreme that they name: `sample_counts`: each brick and strip has a level of at most 16; its rays take 1 to that level samples; some brick and strip reaches 16. `brick_rank`: each row is a permutation of the bricks.
All inputs are finite; a program needn't handle non-finite values.
Results may differ from a plain program's by a relative error of at most 0.015.
Values may be sent and summed in bfloat16 or wider, within the bound.
A program may use at most 64 MiB of HBM per device.

v0:
```python
import math
import jax
import jax.numpy as jnp
from jax import lax
from jax.sharding import PartitionSpec as P

SAMPLES = 16
ROWS_OWN = 16
COLS_DEV = 16


def padded_2(x, sides, width):
    for axis, dim in sides:
        size, length = (lax.axis_size(axis), x.shape[dim])
        up = [(i, (i + 1) % size) for i in range(size - 1)]
        down = [(j, i) for i, j in up]
        last = lax.slice_in_dim(x, length - width, length, axis=dim)
        first = lax.slice_in_dim(x, 0, width, axis=dim)
        before = lax.ppermute(last, axis, up)
        after = lax.ppermute(first, axis, down)
        x = jnp.concatenate([before, x, after], axis=dim)
    return x


def blend_sample_values(field, counts, bricks):
    step_len = 8.0 / (SAMPLES * bricks)
    slot_ids = jnp.arange(SAMPLES, dtype=jnp.int32)
    valid = (slot_ids[:, None] < counts[None, :]).astype(jnp.float32)
    optical = step_len * jax.nn.softplus(field[0]) * valid
    earlier = (slot_ids[:, None] > slot_ids[None, :]).astype(jnp.float32)
    before = jnp.dot(earlier, optical, precision=lax.Precision.HIGHEST)
    weights = jnp.exp(-before) * (1.0 - jnp.exp(-optical))
    colour = jnp.sum(weights[None] * field[1:], axis=1)
    return (colour, jnp.sum(optical, axis=0))


def convolve_valid(padded, weights):
    height = padded.shape[0] - 2
    width = padded.shape[1] - 2
    total = jnp.zeros((height * width, weights.shape[2]), jnp.float32)
    for tap in range(9):
        row_offset_shift, shift_col = divmod(tap, 3)
        window = padded[
            row_offset_shift : row_offset_shift + height, shift_col : shift_col + width
        ].reshape(height * width, -1)
        total = total + jnp.dot(window, weights[tap], preferred_element_type=jnp.float32)
    return total.reshape(height, width, weights.shape[2])


def border_padding(source):
    return padded_2(source, (("depth", 0), ("rays", 1)), 1)


def shards(
    brick_features,
    entry_cells,
    sample_counts,
    brick_rank,
    input_layer_weight,
    second_weight,
    conv_in,
    conv_mid,
    conv_out,
):
    bricks = lax.axis_size("depth")
    feat_count = brick_features.shape[0]
    cell_count = brick_features.shape[3]
    windows = cell_count // SAMPLES
    span = SAMPLES * feat_count
    table = (
        brick_features.reshape(feat_count, windows, SAMPLES)
        .transpose(1, 2, 0)
        .reshape(windows, span)
    )
    entries = entry_cells.reshape(-1)
    counts = sample_counts.reshape(-1)
    ranks = brick_rank.reshape(-1)
    total_rays = entries.shape[0]
    block = math.gcd(total_rays, 512)
    shift_bits = (SAMPLES - 1).bit_length()

    def march_block(operands):
        block_entries, block_counts = operands
        window_ids = block_entries // SAMPLES
        offset = block_entries - window_ids * SAMPLES
        following = jnp.minimum(window_ids + 1, windows - 1)
        paired = jnp.concatenate(
            [jnp.take(table, window_ids, axis=0), jnp.take(table, following, axis=0)], axis=1
        )
        for level in range(shift_bits):
            moved_by = (1 << level) * feat_count
            moved = jnp.concatenate(
                [paired[:, moved_by:], jnp.zeros((block, moved_by), paired.dtype)], axis=1
            )
            taken = (offset >> level & 1)[:, None] == 1
            paired = jnp.where(taken, moved, paired)
        probed_values = paired[:, :span].reshape(block, SAMPLES, feat_count)
        before_activation = jnp.einsum(
            "fh,isf->hsi", input_layer_weight, probed_values, preferred_element_type=jnp.float32
        )
        hidden = (
            jnp.maximum(before_activation, 0.0).astype(jnp.bfloat16).reshape(-1, SAMPLES * block)
        )
        field = jnp.einsum("ho,hn->on", second_weight, hidden, preferred_element_type=jnp.float32)
        return blend_sample_values(field.reshape(-1, SAMPLES, block), block_counts, bricks)

    colour_blocks, depth_blocks = lax.map(
        march_block, (entries.reshape(-1, block), counts.reshape(-1, block))
    )
    colour = jnp.transpose(colour_blocks, (1, 0, 2)).reshape(colour_blocks.shape[1], total_rays)
    depth_sum = depth_blocks.reshape(1, total_rays)
    all_depth = lax.all_gather(depth_sum, "depth", axis=0, tiled=True)
    my_rank = ranks[lax.axis_index("depth")]
    ahead = (ranks < my_rank).astype(jnp.float32)[None, :]
    front = jnp.dot(ahead, all_depth, precision=lax.Precision.HIGHEST)
    image = lax.psum_scatter(
        (colour * jnp.exp(-front)).astype(jnp.bfloat16), "depth", scatter_dimension=1, tiled=True
    ).astype(jnp.float32)
    image = image.reshape(-1, ROWS_OWN, COLS_DEV).transpose(1, 2, 0).astype(jnp.bfloat16)
    first = jnp.maximum(convolve_valid(border_padding(image), conv_in), 0.0).astype(jnp.bfloat16)
    second = jnp.maximum(convolve_valid(border_padding(first), conv_mid), 0.0).astype(jnp.bfloat16)
    frame = convolve_valid(border_padding(second), conv_out).astype(jnp.bfloat16)
    return frame


def solution(mesh):
    placed = (
        P(None, ("groups", "depth"), "rays", None),
        P(("groups", "depth"), "rays", None),
        P(("groups", "depth"), "rays", None),
        P(("groups", "rays"), None),
        P(),
        P(),
        P(),
        P(),
        P(),
    )
    return jax.shard_map(
        shards,
        mesh=mesh,
        in_specs=placed,
        out_specs=P(("groups", "depth"), "rays", None),
        check_vma=False,
    )
```

profile of v0, /device:TPU:1, one launch (start us, length us, event | category | flops | bytes accessed | tf_op | source)
XLA Modules:
  0.0 133.9 jit_solution(3947614905401499600)
XLA Ops:
  9.6 5.4 %reshape.274 = bf16[16,1024,16]{2,1,0:T(8,128)(2,1)} reshape(bf16[16,1,1,16384]{3,0,2,1:T(8,128)(2,1)} %param.13) | data formatting | bytes 1048576 | tf_op jit(solution)/shard_map/reshape | solution.py:71
  15.1 3.7 %copy.18 = bf16[1024,16,16]{0,2,1:T(8,128)(2,1)S(1)} copy(bf16[1024,16,16]{1,0,2:T(8,128)(2,1)} %bitcast.218) | data formatting | bytes 1048576 | tf_op jit(solution)/shard_map/transpose | solution.py:72
  19.0 19.6 %while.14 = (s32[]{:T(128)}, f32[2,32,512]{2,1,0:T(8,128)S(1)}, f32[2,512]{1,0:T(2,128)S(1)}, s32[2,512]{1,0:T(2,128)S(1)}, s32[2,512]{1,0:T(2,128)S(1)}, /*inde...) while((s32[]{:T(128)}, f32[2,32,512]{2,1,0:T(8,128)S(1)}, ...), condition=%wide.region_3.5_spmd, body=%wide.region_0.4_spmd.sunk | while | flops 110472448 | bytes 23171440 | solution.py:107
  19.1 2.0 %gather_fusion.1 = bf16[512,256]{1,0:T(8,128)(2,1)S(1)} fusion(bf16[1024,256]{1,0:T(8,128)(2,1)S(1)} %get-tuple-element.298, s32[1024]{0:T(1024)S(1)} %pad_clamp_fusion.5), kind=kCustom, calls=%fused_computation.clone.clone.1 | custom fusion | bytes 526336 | tf_op jit(solution)/shard_map/while/body/eval_jaxpr/jit(_take)/gather | solution.py:88
  21.2 2.0 %gather_fusion = bf16[512,256]{1,0:T(8,128)(2,1)S(1)} fusion(bf16[1024,256]{1,0:T(8,128)(2,1)S(1)} %get-tuple-element.298, s32[1024]{0:T(1024)S(1)} %pad_clamp_fusion.4), kind=kCustom, calls=%fused_computation.1.clone.clone.1 | custom fusion | bytes 526336 | tf_op jit(solution)/shard_map/while/body/eval_jaxpr/jit(_take)/gather | solution.py:88
  26.1 1.3 convolution_bitcast_fusion.2
  28.9 2.0 %gather_fusion.1 = bf16[512,256]{1,0:T(8,128)(2,1)S(1)} fusion(bf16[1024,256]{1,0:T(8,128)(2,1)S(1)} %get-tuple-element.298, s32[1024]{0:T(1024)S(1)} %pad_clamp_fusion.5), kind=kCustom, calls=%fused_computation.clone.clone.1 | custom fusion | bytes 526336 | tf_op jit(solution)/shard_map/while/body/eval_jaxpr/jit(_take)/gather | solution.py:88
  31.0 2.0 %gather_fusion = bf16[512,256]{1,0:T(8,128)(2,1)S(1)} fusion(bf16[1024,256]{1,0:T(8,128)(2,1)S(1)} %get-tuple-element.298, s32[1024]{0:T(1024)S(1)} %pad_clamp_fusion.4), kind=kCustom, calls=%fused_computation.1.clone.clone.1 | custom fusion | bytes 526336 | tf_op jit(solution)/shard_map/while/body/eval_jaxpr/jit(_take)/gather | solution.py:88
  38.6 11.3 %all-gather = f32[4,1,1024]{2,1,0:T(1,128)S(1)} all-gather(f32[1,1,1024]{2,1,0:T(1,128)S(1)} %reshape.322), channel_id=1, replica_groups=mesh['groups'=2,'depth'=4,'rays'=4] {'depth'}, dimensions={0}, use_global_device_ids=true | all-gather | bytes 20480 | tf_op jit(solution)/shard_map/all_gather | solution.py:112
  52.0 20.8 %reduce-scatter.2.cloned.1.call-done = bf16[32,256]{1,0:T(8,128)(2,1)} async-done(((bf16[32,1024]{1,0:T(8,128)(2,1)}), bf16[32,256]{1,0:T(8,128)(2,1)}) %reduce-scatter.2.cloned.1.call-update) | async-done | bytes 16400 | tf_op jit(solution)/shard_map/reduce_scatter | solution.py:116
  76.2 3.0 %collective-permute-done.1 = bf16[1,16,32]{2,1,0:T(8,128)(2,1)S(1)} collective-permute-done((bf16[1,16,32]{2,1,0:T(8,128)(2,1)S(1)}, bf16[1,16,32]{2,1,0:T(8,128)(2,1)S(1)}, u32[]{:S(2)}, u32[]{:S(2)}) %collective-permute-start.1) | collective-permute-done | bytes 1056 | tf_op jit(solution)/shard_map/ppermute | solution.py:20
  79.3 7.1 %collective-permute-start.2 = (bf16[18,1,32]{2,1,0:T(2,128)(2,1)S(1)}, bf16[18,1,32]{2,1,0:T(2,128)(2,1)S(1)}, u32[]{:S(2)}, u32[]{:S(2)}) collective-permute-start(bf16[18,1,32]{2,1,0:T(2,128)(2,1)S(1)} %get-tuple-element.183), channel_id=1, source_target_pairs={{0,1},{1,2},{2,3},{4,5},{5,6},{6,7},{8,9},{9,10},{10,11},{12,13},{... | collective-permute-start | bytes 3464 | tf_op jit(solution)/shard_map/ppermute | solution.py:19
  86.4 1.9 %collective-permute-start.3 = (bf16[18,1,32]{2,1,0:T(2,128)(2,1)S(1)}, bf16[18,1,32]{2,1,0:T(2,128)(2,1)S(1)}, u32[]{:S(2)}, u32[]{:S(2)}) collective-permute-start(bf16[18,1,32]{2,1,0:T(2,128)(2,1)S(1)} %get-tuple-element.184), channel_id=1, source_target_pairs={{1,0},{2,1},{3,2},{5,4},{6,5},{7,6},{9,8},{10,9},{11,10},{13,12},{... | collective-permute-start | bytes 3464 | tf_op jit(solution)/shard_map/ppermute | solution.py:20
  88.5 2.9 %collective-permute-done.3 = bf16[18,1,32]{2,1,0:T(2,128)(2,1)S(1)} collective-permute-done((bf16[18,1,32]{2,1,0:T(2,128)(2,1)S(1)}, bf16[18,1,32]{2,1,0:T(2,128)(2,1)S(1)}, u32[]{:S(2)}, u32[]{:S(2)}) %collective-permute-start.3) | collective-permute-done | bytes 1184 | tf_op jit(solution)/shard_map/ppermute | solution.py:20
  92.7 3.4 %collective-permute-start.4 = (bf16[1,16,128]{2,1,0:T(8,128)(2,1)S(1)}, bf16[1,16,128]{2,1,0:T(8,128)(2,1)S(1)}, u32[]{:S(2)}, u32[]{:S(2)}) collective-permute-start(bf16[1,16,128]{2,1,0:T(8,128)(2,1)S(1)} %get-tuple-element.191), channel_id=1, source_target_pairs={{0,4},{4,8},{8,12},{1,5},{5,9},{9,13},{2,6},{6,10},{10,14},{3,7},{... | collective-permute-start | bytes 12296 | tf_op jit(solution)/shard_map/ppermute | solution.py:19
  97.4 3.0 %collective-permute-done.5 = bf16[1,16,128]{2,1,0:T(8,128)(2,1)S(1)} collective-permute-done((bf16[1,16,128]{2,1,0:T(8,128)(2,1)S(1)}, bf16[1,16,128]{2,1,0:T(8,128)(2,1)S(1)}, u32[]{:S(2)}, u32[]{:S(2)}) %collective-permute-start.5) | collective-permute-done | bytes 4128 | tf_op jit(solution)/shard_map/ppermute | solution.py:20
  100.4 3.4 %collective-permute-start.6 = (bf16[18,1,128]{2,1,0:T(2,128)(2,1)S(1)}, bf16[18,1,128]{2,1,0:T(2,128)(2,1)S(1)}, u32[]{:S(2)}, u32[]{:S(2)}) collective-permute-start(bf16[18,1,128]{2,1,0:T(2,128)(2,1)S(1)} %get-tuple-element.179), channel_id=1, source_target_pairs={{0,1},{1,2},{2,3},{4,5},{5,6},{6,7},{8,9},{9,10},{10,11},{12,13},{... | collective-permute-start | bytes 13832 | tf_op jit(solution)/shard_map/ppermute | solution.py:19
  103.8 1.9 %collective-permute-start.7 = (bf16[18,1,128]{2,1,0:T(2,128)(2,1)S(1)}, bf16[18,1,128]{2,1,0:T(2,128)(2,1)S(1)}, u32[]{:S(2)}, u32[]{:S(2)}) collective-permute-start(bf16[18,1,128]{2,1,0:T(2,128)(2,1)S(1)} %get-tuple-element.180), channel_id=1, source_target_pairs={{1,0},{2,1},{3,2},{5,4},{6,5},{7,6},{9,8},{10,9},{11,10},{13,12},{... | collective-permute-start | bytes 13832 | tf_op jit(solution)/shard_map/ppermute | solution.py:20
  106.0 2.9 %collective-permute-done.7 = bf16[18,1,128]{2,1,0:T(2,128)(2,1)S(1)} collective-permute-done((bf16[18,1,128]{2,1,0:T(2,128)(2,1)S(1)}, bf16[18,1,128]{2,1,0:T(2,128)(2,1)S(1)}, u32[]{:S(2)}, u32[]{:S(2)}) %collective-permute-start.7) | collective-permute-done | bytes 4640 | tf_op jit(solution)/shard_map/ppermute | solution.py:20
  110.2 2.1 %collective-permute-start.8 = (bf16[1,16,128]{2,1,0:T(8,128)(2,1)S(1)}, bf16[1,16,128]{2,1,0:T(8,128)(2,1)S(1)}, u32[]{:S(2)}, u32[]{:S(2)}) collective-permute-start(bf16[1,16,128]{2,1,0:T(8,128)(2,1)S(1)} %get-tuple-element.187), channel_id=1, source_target_pairs={{0,4},{4,8},{8,12},{1,5},{5,9},{9,13},{2,6},{6,10},{10,14},{3,7},{... | collective-permute-start | bytes 12296 | tf_op jit(solution)/shard_map/ppermute | solution.py:19
  113.6 3.0 %collective-permute-done.9 = bf16[1,16,128]{2,1,0:T(8,128)(2,1)S(1)} collective-permute-done((bf16[1,16,128]{2,1,0:T(8,128)(2,1)S(1)}, bf16[1,16,128]{2,1,0:T(8,128)(2,1)S(1)}, u32[]{:S(2)}, u32[]{:S(2)}) %collective-permute-start.9) | collective-permute-done | bytes 4128 | tf_op jit(solution)/shard_map/ppermute | solution.py:20
  116.7 3.4 %collective-permute-start.10 = (bf16[18,1,128]{2,1,0:T(2,128)(2,1)S(1)}, bf16[18,1,128]{2,1,0:T(2,128)(2,1)S(1)}, u32[]{:S(2)}, u32[]{:S(2)}) collective-permute-start(bf16[18,1,128]{2,1,0:T(2,128)(2,1)S(1)} %get-tuple-element.175), channel_id=1, source_target_pairs={{0,1},{1,2},{2,3},{4,5},{5,6},{6,7},{8,9},{9,10},{10,11},{12,13},{... | collective-permute-start | bytes 13832 | tf_op jit(solution)/shard_map/ppermute | solution.py:19
  120.1 1.9 %collective-permute-start.11 = (bf16[18,1,128]{2,1,0:T(2,128)(2,1)S(1)}, bf16[18,1,128]{2,1,0:T(2,128)(2,1)S(1)}, u32[]{:S(2)}, u32[]{:S(2)}) collective-permute-start(bf16[18,1,128]{2,1,0:T(2,128)(2,1)S(1)} %get-tuple-element.176), channel_id=1, source_target_pairs={{1,0},{2,1},{3,2},{5,4},{6,5},{7,6},{9,8},{10,9},{11,10},{13,12},{... | collective-permute-start | bytes 13832 | tf_op jit(solution)/shard_map/ppermute | solution.py:20
  122.2 2.9 %collective-permute-done.11 = bf16[18,1,128]{2,1,0:T(2,128)(2,1)S(1)} collective-permute-done((bf16[18,1,128]{2,1,0:T(2,128)(2,1)S(1)}, bf16[18,1,128]{2,1,0:T(2,128)(2,1)S(1)}, u32[]{:S(2)}, u32[]{:S(2)}) %collective-permute-start.11) | collective-permute-done | bytes 4640 | tf_op jit(solution)/shard_map/ppermute | solution.py:20
  (140 shorter events, 26.4 us)
Async XLA Ops:
  6.5 66.3 %reduce-scatter.2.cloned.1.call-start = ((), (), s32[]{:S(2)}) async-start(), calls=%async_computation.1 | async-start | bytes 81920 | tf_op jit(solution)/shard_map/reduce_scatter | solution.py:116
  15.1 3.9 %copy-start.2 = (bf16[128,33]{0,1:T(8,128)(2,1)S(1)}, bf16[128,33]{0,1:T(8,128)(2,1)}, u32[]{:S(2)}) copy-start(bf16[128,33]{0,1:T(8,128)(2,1)} %param.18) | copy-start | bytes 25348
  15.1 3.9 %copy-start.3 = (bf16[16,128]{1,0:T(8,128)(2,1)S(1)}, bf16[16,128]{1,0:T(8,128)(2,1)}, u32[]{:S(2)}) copy-start(bf16[16,128]{1,0:T(8,128)(2,1)} %param.17) | copy-start | bytes 12292
  19.0 30.9 %copy-start.5 = (s32[1,4]{1,0:T(1,128)S(1)}, s32[1,4]{1,0:T(1,128)}, u32[]{:S(2)}) copy-start(s32[1,4]{1,0:T(1,128)} %param.16) | copy-start | bytes 52
  19.0 69.4 %copy-start.4 = (bf16[9,32,128]{2,1,0:T(8,128)(2,1)S(1)}, bf16[9,32,128]{2,1,0:T(8,128)(2,1)}, u32[]{:S(2)}) copy-start(bf16[9,32,128]{2,1,0:T(8,128)(2,1)} %param.19) | copy-start | bytes 221188
  73.6 2.6 %collective-permute-start = (bf16[1,16,32]{2,1,0:T(8,128)(2,1)S(1)}, bf16[1,16,32]{2,1,0:T(8,128)(2,1)S(1)}, u32[]{:S(2)}, u32[]{:S(2)}) collective-permute-start(bf16[1,16,32]{2,1,0:T(8,128)(2,1)S(1)} %get-tuple-element.195), channel_id=1, source_target_pairs={{0,4},{4,8},{8,12},{1,5},{5,9},{9,13},{2,6},{6,10},{10,14},{3,7},{... | collective-permute-start | bytes 3080 | tf_op jit(solution)/shard_map/ppermute | solution.py:19
  74.9 4.4 %collective-permute-start.1 = (bf16[1,16,32]{2,1,0:T(8,128)(2,1)S(1)}, bf16[1,16,32]{2,1,0:T(8,128)(2,1)S(1)}, u32[]{:S(2)}, u32[]{:S(2)}) collective-permute-start(bf16[1,16,32]{2,1,0:T(8,128)(2,1)S(1)} %get-tuple-element.196), channel_id=1, source_target_pairs={{4,0},{8,4},{12,8},{5,1},{9,5},{13,9},{6,2},{10,6},{14,10},{7,3},{... | collective-permute-start | bytes 3080 | tf_op jit(solution)/shard_map/ppermute | solution.py:20
  79.3 9.2 %collective-permute-start.2 = (bf16[18,1,32]{2,1,0:T(2,128)(2,1)S(1)}, bf16[18,1,32]{2,1,0:T(2,128)(2,1)S(1)}, u32[]{:S(2)}, u32[]{:S(2)}) collective-permute-start(bf16[18,1,32]{2,1,0:T(2,128)(2,1)S(1)} %get-tuple-element.183), channel_id=1, source_target_pairs={{0,1},{1,2},{2,3},{4,5},{5,6},{6,7},{8,9},{9,10},{10,11},{12,13},{... | collective-permute-start | bytes 3464 | tf_op jit(solution)/shard_map/ppermute | solution.py:19
  86.4 5.0 %collective-permute-start.3 = (bf16[18,1,32]{2,1,0:T(2,128)(2,1)S(1)}, bf16[18,1,32]{2,1,0:T(2,128)(2,1)S(1)}, u32[]{:S(2)}, u32[]{:S(2)}) collective-permute-start(bf16[18,1,32]{2,1,0:T(2,128)(2,1)S(1)} %get-tuple-element.184), channel_id=1, source_target_pairs={{1,0},{2,1},{3,2},{5,4},{6,5},{7,6},{9,8},{10,9},{11,10},{13,12},{... | collective-permute-start | bytes 3464 | tf_op jit(solution)/shard_map/ppermute | solution.py:20
  88.4 17.4 %copy-start = (bf16[9,128,128]{2,1,0:T(8,128)(2,1)S(1)}, bf16[9,128,128]{2,1,0:T(8,128)(2,1)}, u32[]{:S(2)}) copy-start(bf16[9,128,128]{2,1,0:T(8,128)(2,1)} %param.20) | copy-start | bytes 884740
  92.7 4.7 %collective-permute-start.4 = (bf16[1,16,128]{2,1,0:T(8,128)(2,1)S(1)}, bf16[1,16,128]{2,1,0:T(8,128)(2,1)S(1)}, u32[]{:S(2)}, u32[]{:S(2)}) collective-permute-start(bf16[1,16,128]{2,1,0:T(8,128)(2,1)S(1)} %get-tuple-element.191), channel_id=1, source_target_pairs={{0,4},{4,8},{8,12},{1,5},{5,9},{9,13},{2,6},{6,10},{10,14},{3,7},{... | collective-permute-start | bytes 12296 | tf_op jit(solution)/shard_map/ppermute | solution.py:19
  96.1 4.4 %collective-permute-start.5 = (bf16[1,16,128]{2,1,0:T(8,128)(2,1)S(1)}, bf16[1,16,128]{2,1,0:T(8,128)(2,1)S(1)}, u32[]{:S(2)}, u32[]{:S(2)}) collective-permute-start(bf16[1,16,128]{2,1,0:T(8,128)(2,1)S(1)} %get-tuple-element.192), channel_id=1, source_target_pairs={{4,0},{8,4},{12,8},{5,1},{9,5},{13,9},{6,2},{10,6},{14,10},{7,3},{... | collective-permute-start | bytes 12296 | tf_op jit(solution)/shard_map/ppermute | solution.py:20
  100.4 5.5 %collective-permute-start.6 = (bf16[18,1,128]{2,1,0:T(2,128)(2,1)S(1)}, bf16[18,1,128]{2,1,0:T(2,128)(2,1)S(1)}, u32[]{:S(2)}, u32[]{:S(2)}) collective-permute-start(bf16[18,1,128]{2,1,0:T(2,128)(2,1)S(1)} %get-tuple-element.179), channel_id=1, source_target_pairs={{0,1},{1,2},{2,3},{4,5},{5,6},{6,7},{8,9},{9,10},{10,11},{12,13},{... | collective-permute-start | bytes 13832 | tf_op jit(solution)/shard_map/ppermute | solution.py:19
  103.8 5.0 %collective-permute-start.7 = (bf16[18,1,128]{2,1,0:T(2,128)(2,1)S(1)}, bf16[18,1,128]{2,1,0:T(2,128)(2,1)S(1)}, u32[]{:S(2)}, u32[]{:S(2)}) collective-permute-start(bf16[18,1,128]{2,1,0:T(2,128)(2,1)S(1)} %get-tuple-element.180), channel_id=1, source_target_pairs={{1,0},{2,1},{3,2},{5,4},{6,5},{7,6},{9,8},{10,9},{11,10},{13,12},{... | collective-permute-start | bytes 13832 | tf_op jit(solution)/shard_map/ppermute | solution.py:20
  105.9 16.1 %copy-start.1 = (bf16[9,128,128]{2,1,0:T(8,128)(2,1)S(1)}, bf16[9,128,128]{2,1,0:T(8,128)(2,1)}, u32[]{:S(2)}) copy-start(bf16[9,128,128]{2,1,0:T(8,128)(2,1)} %param.21) | copy-start | bytes 884740
  110.2 3.5 %collective-permute-start.8 = (bf16[1,16,128]{2,1,0:T(8,128)(2,1)S(1)}, bf16[1,16,128]{2,1,0:T(8,128)(2,1)S(1)}, u32[]{:S(2)}, u32[]{:S(2)}) collective-permute-start(bf16[1,16,128]{2,1,0:T(8,128)(2,1)S(1)} %get-tuple-element.187), channel_id=1, source_target_pairs={{0,4},{4,8},{8,12},{1,5},{5,9},{9,13},{2,6},{6,10},{10,14},{3,7},{... | collective-permute-start | bytes 12296 | tf_op jit(solution)/shard_map/ppermute | solution.py:19
  112.3 4.4 %collective-permute-start.9 = (bf16[1,16,128]{2,1,0:T(8,128)(2,1)S(1)}, bf16[1,16,128]{2,1,0:T(8,128)(2,1)S(1)}, u32[]{:S(2)}, u32[]{:S(2)}) collective-permute-start(bf16[1,16,128]{2,1,0:T(8,128)(2,1)S(1)} %get-tuple-element.188), channel_id=1, source_target_pairs={{4,0},{8,4},{12,8},{5,1},{9,5},{13,9},{6,2},{10,6},{14,10},{7,3},{... | collective-permute-start | bytes 12296 | tf_op jit(solution)/shard_map/ppermute | solution.py:20
  116.7 5.5 %collective-permute-start.10 = (bf16[18,1,128]{2,1,0:T(2,128)(2,1)S(1)}, bf16[18,1,128]{2,1,0:T(2,128)(2,1)S(1)}, u32[]{:S(2)}, u32[]{:S(2)}) collective-permute-start(bf16[18,1,128]{2,1,0:T(2,128)(2,1)S(1)} %get-tuple-element.175), channel_id=1, source_target_pairs={{0,1},{1,2},{2,3},{4,5},{5,6},{6,7},{8,9},{9,10},{10,11},{12,13},{... | collective-permute-start | bytes 13832 | tf_op jit(solution)/shard_map/ppermute | solution.py:19
  120.1 5.0 %collective-permute-start.11 = (bf16[18,1,128]{2,1,0:T(2,128)(2,1)S(1)}, bf16[18,1,128]{2,1,0:T(2,128)(2,1)S(1)}, u32[]{:S(2)}, u32[]{:S(2)}) collective-permute-start(bf16[18,1,128]{2,1,0:T(2,128)(2,1)S(1)} %get-tuple-element.176), channel_id=1, source_target_pairs={{1,0},{2,1},{3,2},{5,4},{6,5},{7,6},{9,8},{10,9},{11,10},{13,12},{... | collective-permute-start | bytes 13832 | tf_op jit(solution)/shard_map/ppermute | solution.py:20
Sparse Core Ops, SparseCore 0:
  52.1 20.6 reduce-scatter.1
where the time goes:
time: 135 us; the launch traced here: 134 us
  waiting for transfers between devices  38.6 us (29%)
  starting transfers between devices  30.3 us (22%)
  local copies, waits for them, and re-layouts  22.4 us (17%)
  between operations  13.9 us (10%)
  blocking collectives  11.3 us (8%)
  matrix products  9.79 us (7%)
  other arithmetic  7.22 us (5%)
    reduce_scatter x1, waiting for transfers between devices, shards(): lax.psum_scatter((colour * jnp.exp(-front)).astype(jnp.bfloat16), 'depth'...  20.8 us
    ppermute x6, starting transfers between devices, padded_2(): before = lax.ppermute(last, axis, up)  20.7 us
    ppermute x6, waiting for transfers between devices, padded_2(): after = lax.ppermute(first, axis, down)  17.7 us
    all_gather x1, blocking collectives, shards(): all_depth = lax.all_gather(depth_sum, 'depth', axis=0, tiled=True)  11.3 us
    ppermute x6, starting transfers between devices, padded_2(): after = lax.ppermute(first, axis, down)  9.64 us
    reshape x1, local copies, waits for them, and re-layouts, shards(): brick_features.reshape(feat_count, windows, SAMPLES).transpose(1, 2, 0)  5.43 us
    dot_general x27, matrix products, convolve_valid(): jnp.dot(window, weights[tap], preferred_element_type=jnp.float32)  4.52 us
    gather x2, local copies, waits for them, and re-layouts, march_block(): jnp.take(table, following, axis=0)  3.91 us
  transfers between devices with their start and end apart: 13, of which 7 were waited for; matrix products, arithmetic and copies ran while one was open for 0% of the time, Pallas kernels for 0%

commit v1 on v0

--- a/solution.py
+++ b/solution.py
@@ -7,6 +7,18 @@
 SAMPLES = 16
 ROWS_OWN = 16
 COLS_DEV = 16
+
+
+def gather_by_bits(x, axis, dim):
+    ways, here = (lax.axis_size(axis), lax.axis_index(axis))
+    grown, reach = (x, 1)
+    while reach < ways:
+        theirs = lax.ppermute(grown, axis, [(d, d ^ reach) for d in range(ways)])
+        mine_first = jnp.concatenate([grown, theirs], axis=dim)
+        theirs_first = jnp.concatenate([theirs, grown], axis=dim)
+        grown = jnp.where(here & reach == 0, mine_first, theirs_first)
+        reach = 2 * reach
+    return grown
 
 
 def padded_2(x, sides, width):
@@ -109,7 +121,7 @@
     )
     colour = jnp.transpose(colour_blocks, (1, 0, 2)).reshape(colour_blocks.shape[1], total_rays)
     depth_sum = depth_blocks.reshape(1, total_rays)
-    all_depth = lax.all_gather(depth_sum, "depth", axis=0, tiled=True)
+    all_depth = gather_by_bits(depth_sum, "depth", 0)
     my_rank = ranks[lax.axis_index("depth")]
     ahead = (ranks < my_rank).astype(jnp.float32)[None, :]
     front = jnp.dot(ahead, all_depth, precision=lax.Precision.HIGHEST)

time: 135 us -> 129 us (0.956)
  blocking collectives: 11.3 us -> 0 us
  starting transfers between devices: 30.3 us -> 35 us
    all_gather x1 -> x0, blocking collectives: 11.3 us -> none  [shards(): all_depth = lax.all_gather(depth_sum, 'depth', axis=0, tiled=True)]
    ppermute x0 -> x2, starting transfers between devices: none -> 4.73 us  [gather_by_bits(): theirs = lax.ppermute(grown, axis, [(d, d ^ reach) for d in range(ways)])]
    ppermute x0 -> x2, waiting for transfers between devices: none -> 1.43 us  [gather_by_bits(): theirs = lax.ppermute(grown, axis, [(d, d ^ reach) for d in range(ways)])]
  transfers between devices with their start and end apart: 13 -> 15, of which waited for: 7 -> 9; matrix products, arithmetic and copies ran while one was open for 0% -> 1% of each run, Pallas kernels for 0% -> 0%
where the time goes in v1:
time: 129 us
  waiting for transfers between devices  39.7 us (31%)
  starting transfers between devices  35 us (27%)
  local copies, waits for them, and re-layouts  22.5 us (17%)
  between operations  13.9 us (11%)
  matrix products  9.8 us (8%)
  other arithmetic  7.46 us (6%)
    ppermute x6, starting transfers between devices, padded_2(): before = lax.ppermute(last, axis, up)  20.6 us
    reduce_scatter x1, waiting for transfers between devices, shards(): lax.psum_scatter((colour * jnp.exp(-front)).astype(jnp.bfloat16), 'depth'...  20.5 us
    ppermute x6, waiting for transfers between devices, padded_2(): after = lax.ppermute(first, axis, down)  17.7 us
    ppermute x6, starting transfers between devices, padded_2(): after = lax.ppermute(first, axis, down)  9.64 us
    reshape x1, local copies, waits for them, and re-layouts, shards(): brick_features.reshape(feat_count, windows, SAMPLES).transpose(1, 2, 0)  5.44 us
    ppermute x2, starting transfers between devices, gather_by_bits(): theirs = lax.ppermute(grown, axis, [(d, d ^ reach) for d in range(ways)])  4.73 us
    dot_general x27, matrix products, convolve_valid(): jnp.dot(window, weights[tap], preferred_element_type=jnp.float32)  4.52 us
    gather x2, local copies, waits for them, and re-layouts, march_block(): jnp.take(table, window_ids, axis=0)  3.91 us
  transfers between devices with their start and end apart: 15, of which 9 were waited for; matrix products, arithmetic and copies ran while one was open for 1% of the time, Pallas kernels for 0%

profile of v1, /device:TPU:1, one launch (start us, length us, event | category | flops | bytes accessed | tf_op | source)
XLA Modules:
  0.0 128.7 jit_solution(11361095207159921004)
XLA Ops:
  9.9 5.4 %reshape.274 = bf16[16,1024,16]{2,1,0:T(8,128)(2,1)} reshape(bf16[16,1,1,16384]{3,0,2,1:T(8,128)(2,1)} %param.13) | data formatting | bytes 1048576 | tf_op jit(solution)/shard_map/reshape | solution.py:83
  15.4 3.7 %copy.13 = bf16[1024,16,16]{0,2,1:T(8,128)(2,1)S(1)} copy(bf16[1024,16,16]{1,0,2:T(8,128)(2,1)} %bitcast.218) | data formatting | bytes 1048576 | tf_op jit(solution)/shard_map/transpose | solution.py:84
  19.3 19.6 %while.14 = (s32[]{:T(128)}, f32[2,32,512]{2,1,0:T(8,128)S(1)}, f32[2,512]{1,0:T(2,128)S(1)}, s32[2,512]{1,0:T(2,128)S(1)}, s32[2,512]{1,0:T(2,128)S(1)}, /*inde...) while((s32[]{:T(128)}, f32[2,32,512]{2,1,0:T(8,128)S(1)}, ...), condition=%wide.region_3.5_spmd, body=%wide.region_0.4_spmd.sunk | while | flops 110472448 | bytes 23171440 | solution.py:119
  19.4 2.0 %gather_fusion.1 = bf16[512,256]{1,0:T(8,128)(2,1)S(1)} fusion(bf16[1024,256]{1,0:T(8,128)(2,1)S(1)} %get-tuple-element.290, s32[1024]{0:T(1024)S(1)} %pad_clamp_fusion.5), kind=kCustom, calls=%fused_computation.clone.clone.1 | custom fusion | bytes 526336 | tf_op jit(solution)/shard_map/while/body/eval_jaxpr/jit(_take)/gather | solution.py:100
  21.5 2.0 %gather_fusion = bf16[512,256]{1,0:T(8,128)(2,1)S(1)} fusion(bf16[1024,256]{1,0:T(8,128)(2,1)S(1)} %get-tuple-element.290, s32[1024]{0:T(1024)S(1)} %pad_clamp_fusion.4), kind=kCustom, calls=%fused_computation.1.clone.clone.1 | custom fusion | bytes 526336 | tf_op jit(solution)/shard_map/while/body/eval_jaxpr/jit(_take)/gather | solution.py:100
  29.2 2.0 %gather_fusion.1 = bf16[512,256]{1,0:T(8,128)(2,1)S(1)} fusion(bf16[1024,256]{1,0:T(8,128)(2,1)S(1)} %get-tuple-element.290, s32[1024]{0:T(1024)S(1)} %pad_clamp_fusion.5), kind=kCustom, calls=%fused_computation.clone.clone.1 | custom fusion | bytes 526336 | tf_op jit(solution)/shard_map/while/body/eval_jaxpr/jit(_take)/gather | solution.py:100
  31.3 2.0 %gather_fusion = bf16[512,256]{1,0:T(8,128)(2,1)S(1)} fusion(bf16[1024,256]{1,0:T(8,128)(2,1)S(1)} %get-tuple-element.290, s32[1024]{0:T(1024)S(1)} %pad_clamp_fusion.4), kind=kCustom, calls=%fused_computation.1.clone.clone.1 | custom fusion | bytes 526336 | tf_op jit(solution)/shard_map/while/body/eval_jaxpr/jit(_take)/gather | solution.py:100
  38.9 2.2 %collective-permute-start = (f32[1,1024]{1,0:T(1,128)S(1)}, f32[1,1024]{1,0:T(1,128)S(1)}, u32[]{:S(2)}, u32[]{:S(2)}) collective-permute-start(f32[1,1024]{1,0:T(1,128)S(1)} %bitcast.260), channel_id=1, source_target_pairs={{0,4},{4,0},{8,12},{12,8},{1,5},{5,1},{9,13},{13,9},{2,6},{6,2},{1... | collective-permute-start | bytes 12296 | tf_op jit(solution)/shard_map/ppermute | solution.py:16
  42.1 2.5 %collective-permute-start.1 = (f32[2,1024]{1,0:T(2,128)S(1)}, f32[2,1024]{1,0:T(2,128)S(1)}, u32[]{:S(2)}, u32[]{:S(2)}) collective-permute-start(f32[2,1024]{1,0:T(2,128)S(1)} %maximum_select_fusion.2), channel_id=1, source_target_pairs={{0,8},{4,12},{8,0},{12,4},{1,9},{5,13},{9,1},{13,5},{2,10},{6,14},... | collective-permute-start | bytes 24584 | tf_op jit(solution)/shard_map/ppermute | solution.py:16
  47.2 20.5 %reduce-scatter.2.cloned.1.call-done = bf16[32,256]{1,0:T(8,128)(2,1)} async-done(((bf16[32,1024]{1,0:T(8,128)(2,1)}), bf16[32,256]{1,0:T(8,128)(2,1)}) %reduce-scatter.2.cloned.1.call-update) | async-done | bytes 16400 | tf_op jit(solution)/shard_map/reduce_scatter | solution.py:128
  71.1 3.0 %collective-permute-done.3 = bf16[1,16,32]{2,1,0:T(8,128)(2,1)S(1)} collective-permute-done((bf16[1,16,32]{2,1,0:T(8,128)(2,1)S(1)}, bf16[1,16,32]{2,1,0:T(8,128)(2,1)S(1)}, u32[]{:S(2)}, u32[]{:S(2)}) %collective-permute-start.3) | collective-permute-done | bytes 1056 | tf_op jit(solution)/shard_map/ppermute | solution.py:32
  74.2 7.1 %collective-permute-start.4 = (bf16[18,1,32]{2,1,0:T(2,128)(2,1)S(1)}, bf16[18,1,32]{2,1,0:T(2,128)(2,1)S(1)}, u32[]{:S(2)}, u32[]{:S(2)}) collective-permute-start(bf16[18,1,32]{2,1,0:T(2,128)(2,1)S(1)} %get-tuple-element.175), channel_id=1, source_target_pairs={{0,1},{1,2},{2,3},{4,5},{5,6},{6,7},{8,9},{9,10},{10,11},{12,13},{... | collective-permute-start | bytes 3464 | tf_op jit(solution)/shard_map/ppermute | solution.py:31
  81.3 1.9 %collective-permute-start.5 = (bf16[18,1,32]{2,1,0:T(2,128)(2,1)S(1)}, bf16[18,1,32]{2,1,0:T(2,128)(2,1)S(1)}, u32[]{:S(2)}, u32[]{:S(2)}) collective-permute-start(bf16[18,1,32]{2,1,0:T(2,128)(2,1)S(1)} %get-tuple-element.176), channel_id=1, source_target_pairs={{1,0},{2,1},{3,2},{5,4},{6,5},{7,6},{9,8},{10,9},{11,10},{13,12},{... | collective-permute-start | bytes 3464 | tf_op jit(solution)/shard_map/ppermute | solution.py:32
  83.4 2.9 %collective-permute-done.5 = bf16[18,1,32]{2,1,0:T(2,128)(2,1)S(1)} collective-permute-done((bf16[18,1,32]{2,1,0:T(2,128)(2,1)S(1)}, bf16[18,1,32]{2,1,0:T(2,128)(2,1)S(1)}, u32[]{:S(2)}, u32[]{:S(2)}) %collective-permute-start.5) | collective-permute-done | bytes 1184 | tf_op jit(solution)/shard_map/ppermute | solution.py:32
  87.5 3.4 %collective-permute-start.6 = (bf16[1,16,128]{2,1,0:T(8,128)(2,1)S(1)}, bf16[1,16,128]{2,1,0:T(8,128)(2,1)S(1)}, u32[]{:S(2)}, u32[]{:S(2)}) collective-permute-start(bf16[1,16,128]{2,1,0:T(8,128)(2,1)S(1)} %get-tuple-element.183), channel_id=1, source_target_pairs={{0,4},{4,8},{8,12},{1,5},{5,9},{9,13},{2,6},{6,10},{10,14},{3,7},{... | collective-permute-start | bytes 12296 | tf_op jit(solution)/shard_map/ppermute | solution.py:31
  92.3 3.0 %collective-permute-done.7 = bf16[1,16,128]{2,1,0:T(8,128)(2,1)S(1)} collective-permute-done((bf16[1,16,128]{2,1,0:T(8,128)(2,1)S(1)}, bf16[1,16,128]{2,1,0:T(8,128)(2,1)S(1)}, u32[]{:S(2)}, u32[]{:S(2)}) %collective-permute-start.7) | collective-permute-done | bytes 4128 | tf_op jit(solution)/shard_map/ppermute | solution.py:32
  95.3 3.4 %collective-permute-start.8 = (bf16[18,1,128]{2,1,0:T(2,128)(2,1)S(1)}, bf16[18,1,128]{2,1,0:T(2,128)(2,1)S(1)}, u32[]{:S(2)}, u32[]{:S(2)}) collective-permute-start(bf16[18,1,128]{2,1,0:T(2,128)(2,1)S(1)} %get-tuple-element.171), channel_id=1, source_target_pairs={{0,1},{1,2},{2,3},{4,5},{5,6},{6,7},{8,9},{9,10},{10,11},{12,13},{... | collective-permute-start | bytes 13832 | tf_op jit(solution)/shard_map/ppermute | solution.py:31
  98.7 1.9 %collective-permute-start.9 = (bf16[18,1,128]{2,1,0:T(2,128)(2,1)S(1)}, bf16[18,1,128]{2,1,0:T(2,128)(2,1)S(1)}, u32[]{:S(2)}, u32[]{:S(2)}) collective-permute-start(bf16[18,1,128]{2,1,0:T(2,128)(2,1)S(1)} %get-tuple-element.172), channel_id=1, source_target_pairs={{1,0},{2,1},{3,2},{5,4},{6,5},{7,6},{9,8},{10,9},{11,10},{13,12},{... | collective-permute-start | bytes 13832 | tf_op jit(solution)/shard_map/ppermute | solution.py:32
  100.8 2.9 %collective-permute-done.9 = bf16[18,1,128]{2,1,0:T(2,128)(2,1)S(1)} collective-permute-done((bf16[18,1,128]{2,1,0:T(2,128)(2,1)S(1)}, bf16[18,1,128]{2,1,0:T(2,128)(2,1)S(1)}, u32[]{:S(2)}, u32[]{:S(2)}) %collective-permute-start.9) | collective-permute-done | bytes 4640 | tf_op jit(solution)/shard_map/ppermute | solution.py:32
  105.1 2.1 %collective-permute-start.10 = (bf16[1,16,128]{2,1,0:T(8,128)(2,1)S(1)}, bf16[1,16,128]{2,1,0:T(8,128)(2,1)S(1)}, u32[]{:S(2)}, u32[]{:S(2)}) collective-permute-start(bf16[1,16,128]{2,1,0:T(8,128)(2,1)S(1)} %get-tuple-element.179), channel_id=1, source_target_pairs={{0,4},{4,8},{8,12},{1,5},{5,9},{9,13},{2,6},{6,10},{10,14},{3,7},{... | collective-permute-start | bytes 12296 | tf_op jit(solution)/shard_map/ppermute | solution.py:31
  108.5 3.0 %collective-permute-done.11 = bf16[1,16,128]{2,1,0:T(8,128)(2,1)S(1)} collective-permute-done((bf16[1,16,128]{2,1,0:T(8,128)(2,1)S(1)}, bf16[1,16,128]{2,1,0:T(8,128)(2,1)S(1)}, u32[]{:S(2)}, u32[]{:S(2)}) %collective-permute-start.11) | collective-permute-done | bytes 4128 | tf_op jit(solution)/shard_map/ppermute | solution.py:32
  111.5 3.4 %collective-permute-start.12 = (bf16[18,1,128]{2,1,0:T(2,128)(2,1)S(1)}, bf16[18,1,128]{2,1,0:T(2,128)(2,1)S(1)}, u32[]{:S(2)}, u32[]{:S(2)}) collective-permute-start(bf16[18,1,128]{2,1,0:T(2,128)(2,1)S(1)} %get-tuple-element.167), channel_id=1, source_target_pairs={{0,1},{1,2},{2,3},{4,5},{5,6},{6,7},{8,9},{9,10},{10,11},{12,13},{... | collective-permute-start | bytes 13832 | tf_op jit(solution)/shard_map/ppermute | solution.py:31
  114.9 1.9 %collective-permute-start.13 = (bf16[18,1,128]{2,1,0:T(2,128)(2,1)S(1)}, bf16[18,1,128]{2,1,0:T(2,128)(2,1)S(1)}, u32[]{:S(2)}, u32[]{:S(2)}) collective-permute-start(bf16[18,1,128]{2,1,0:T(2,128)(2,1)S(1)} %get-tuple-element.168), channel_id=1, source_target_pairs={{1,0},{2,1},{3,2},{5,4},{6,5},{7,6},{9,8},{10,9},{11,10},{13,12},{... | collective-permute-start | bytes 13832 | tf_op jit(solution)/shard_map/ppermute | solution.py:32
  117.0 2.9 %collective-permute-done.13 = bf16[18,1,128]{2,1,0:T(2,128)(2,1)S(1)} collective-permute-done((bf16[18,1,128]{2,1,0:T(2,128)(2,1)S(1)}, bf16[18,1,128]{2,1,0:T(2,128)(2,1)S(1)}, u32[]{:S(2)}, u32[]{:S(2)}) %collective-permute-start.13) | collective-permute-done | bytes 4640 | tf_op jit(solution)/shard_map/ppermute | solution.py:32
  (144 shorter events, 29.5 us)
Async XLA Ops:
  6.5 61.2 %reduce-scatter.2.cloned.1.call-start = ((), (), s32[]{:S(2)}) async-start(), calls=%async_computation.1 | async-start | bytes 81920 | tf_op jit(solution)/shard_map/reduce_scatter | solution.py:128
  15.4 3.9 %copy-start.2 = (bf16[128,33]{0,1:T(8,128)(2,1)S(1)}, bf16[128,33]{0,1:T(8,128)(2,1)}, u32[]{:S(2)}) copy-start(bf16[128,33]{0,1:T(8,128)(2,1)} %param.18) | copy-start | bytes 25348
  15.4 3.9 %copy-start.3 = (bf16[16,128]{1,0:T(8,128)(2,1)S(1)}, bf16[16,128]{1,0:T(8,128)(2,1)}, u32[]{:S(2)}) copy-start(bf16[16,128]{1,0:T(8,128)(2,1)} %param.17) | copy-start | bytes 12292
  19.3 25.4 %copy-start.5 = (s32[1,4]{1,0:T(1,128)S(1)}, s32[1,4]{1,0:T(1,128)}, u32[]{:S(2)}) copy-start(s32[1,4]{1,0:T(1,128)} %param.16) | copy-start | bytes 52
  19.3 63.9 %copy-start.4 = (bf16[9,32,128]{2,1,0:T(8,128)(2,1)S(1)}, bf16[9,32,128]{2,1,0:T(8,128)(2,1)}, u32[]{:S(2)}) copy-start(bf16[9,32,128]{2,1,0:T(8,128)(2,1)} %param.19) | copy-start | bytes 221188
  38.9 3.2 %collective-permute-start = (f32[1,1024]{1,0:T(1,128)S(1)}, f32[1,1024]{1,0:T(1,128)S(1)}, u32[]{:S(2)}, u32[]{:S(2)}) collective-permute-start(f32[1,1024]{1,0:T(1,128)S(1)} %bitcast.260), channel_id=1, source_target_pairs={{0,4},{4,0},{8,12},{12,8},{1,5},{5,1},{9,13},{13,9},{2,6},{6,2},{1... | collective-permute-start | bytes 12296 | tf_op jit(solution)/shard_map/ppermute | solution.py:16
  42.1 3.6 %collective-permute-start.1 = (f32[2,1024]{1,0:T(2,128)S(1)}, f32[2,1024]{1,0:T(2,128)S(1)}, u32[]{:S(2)}, u32[]{:S(2)}) collective-permute-start(f32[2,1024]{1,0:T(2,128)S(1)} %maximum_select_fusion.2), channel_id=1, source_target_pairs={{0,8},{4,12},{8,0},{12,4},{1,9},{5,13},{9,1},{13,5},{2,10},{6,14},... | collective-permute-start | bytes 24584 | tf_op jit(solution)/shard_map/ppermute | solution.py:16
  68.5 2.6 %collective-permute-start.2 = (bf16[1,16,32]{2,1,0:T(8,128)(2,1)S(1)}, bf16[1,16,32]{2,1,0:T(8,128)(2,1)S(1)}, u32[]{:S(2)}, u32[]{:S(2)}) collective-permute-start(bf16[1,16,32]{2,1,0:T(8,128)(2,1)S(1)} %get-tuple-element.187), channel_id=1, source_target_pairs={{0,4},{4,8},{8,12},{1,5},{5,9},{9,13},{2,6},{6,10},{10,14},{3,7},{... | collective-permute-start | bytes 3080 | tf_op jit(solution)/shard_map/ppermute | solution.py:31
  69.8 4.4 %collective-permute-start.3 = (bf16[1,16,32]{2,1,0:T(8,128)(2,1)S(1)}, bf16[1,16,32]{2,1,0:T(8,128)(2,1)S(1)}, u32[]{:S(2)}, u32[]{:S(2)}) collective-permute-start(bf16[1,16,32]{2,1,0:T(8,128)(2,1)S(1)} %get-tuple-element.188), channel_id=1, source_target_pairs={{4,0},{8,4},{12,8},{5,1},{9,5},{13,9},{6,2},{10,6},{14,10},{7,3},{... | collective-permute-start | bytes 3080 | tf_op jit(solution)/shard_map/ppermute | solution.py:32
  74.2 9.2 %collective-permute-start.4 = (bf16[18,1,32]{2,1,0:T(2,128)(2,1)S(1)}, bf16[18,1,32]{2,1,0:T(2,128)(2,1)S(1)}, u32[]{:S(2)}, u32[]{:S(2)}) collective-permute-start(bf16[18,1,32]{2,1,0:T(2,128)(2,1)S(1)} %get-tuple-element.175), channel_id=1, source_target_pairs={{0,1},{1,2},{2,3},{4,5},{5,6},{6,7},{8,9},{9,10},{10,11},{12,13},{... | collective-permute-start | bytes 3464 | tf_op jit(solution)/shard_map/ppermute | solution.py:31
  81.3 5.0 %collective-permute-start.5 = (bf16[18,1,32]{2,1,0:T(2,128)(2,1)S(1)}, bf16[18,1,32]{2,1,0:T(2,128)(2,1)S(1)}, u32[]{:S(2)}, u32[]{:S(2)}) collective-permute-start(bf16[18,1,32]{2,1,0:T(2,128)(2,1)S(1)} %get-tuple-element.176), channel_id=1, source_target_pairs={{1,0},{2,1},{3,2},{5,4},{6,5},{7,6},{9,8},{10,9},{11,10},{13,12},{... | collective-permute-start | bytes 3464 | tf_op jit(solution)/shard_map/ppermute | solution.py:32
  83.3 17.4 %copy-start = (bf16[9,128,128]{2,1,0:T(8,128)(2,1)S(1)}, bf16[9,128,128]{2,1,0:T(8,128)(2,1)}, u32[]{:S(2)}) copy-start(bf16[9,128,128]{2,1,0:T(8,128)(2,1)} %param.20) | copy-start | bytes 884740
  87.5 4.7 %collective-permute-start.6 = (bf16[1,16,128]{2,1,0:T(8,128)(2,1)S(1)}, bf16[1,16,128]{2,1,0:T(8,128)(2,1)S(1)}, u32[]{:S(2)}, u32[]{:S(2)}) collective-permute-start(bf16[1,16,128]{2,1,0:T(8,128)(2,1)S(1)} %get-tuple-element.183), channel_id=1, source_target_pairs={{0,4},{4,8},{8,12},{1,5},{5,9},{9,13},{2,6},{6,10},{10,14},{3,7},{... | collective-permute-start | bytes 12296 | tf_op jit(solution)/shard_map/ppermute | solution.py:31
  91.0 4.4 %collective-permute-start.7 = (bf16[1,16,128]{2,1,0:T(8,128)(2,1)S(1)}, bf16[1,16,128]{2,1,0:T(8,128)(2,1)S(1)}, u32[]{:S(2)}, u32[]{:S(2)}) collective-permute-start(bf16[1,16,128]{2,1,0:T(8,128)(2,1)S(1)} %get-tuple-element.184), channel_id=1, source_target_pairs={{4,0},{8,4},{12,8},{5,1},{9,5},{13,9},{6,2},{10,6},{14,10},{7,3},{... | collective-permute-start | bytes 12296 | tf_op jit(solution)/shard_map/ppermute | solution.py:32
  95.3 5.5 %collective-permute-start.8 = (bf16[18,1,128]{2,1,0:T(2,128)(2,1)S(1)}, bf16[18,1,128]{2,1,0:T(2,128)(2,1)S(1)}, u32[]{:S(2)}, u32[]{:S(2)}) collective-permute-start(bf16[18,1,128]{2,1,0:T(2,128)(2,1)S(1)} %get-tuple-element.171), channel_id=1, source_target_pairs={{0,1},{1,2},{2,3},{4,5},{5,6},{6,7},{8,9},{9,10},{10,11},{12,13},{... | collective-permute-start | bytes 13832 | tf_op jit(solution)/shard_map/ppermute | solution.py:31
  98.7 5.0 %collective-permute-start.9 = (bf16[18,1,128]{2,1,0:T(2,128)(2,1)S(1)}, bf16[18,1,128]{2,1,0:T(2,128)(2,1)S(1)}, u32[]{:S(2)}, u32[]{:S(2)}) collective-permute-start(bf16[18,1,128]{2,1,0:T(2,128)(2,1)S(1)} %get-tuple-element.172), channel_id=1, source_target_pairs={{1,0},{2,1},{3,2},{5,4},{6,5},{7,6},{9,8},{10,9},{11,10},{13,12},{... | collective-permute-start | bytes 13832 | tf_op jit(solution)/shard_map/ppermute | solution.py:32
  100.8 16.1 %copy-start.1 = (bf16[9,128,128]{2,1,0:T(8,128)(2,1)S(1)}, bf16[9,128,128]{2,1,0:T(8,128)(2,1)}, u32[]{:S(2)}) copy-start(bf16[9,128,128]{2,1,0:T(8,128)(2,1)} %param.21) | copy-start | bytes 884740
  105.1 3.4 %collective-permute-start.10 = (bf16[1,16,128]{2,1,0:T(8,128)(2,1)S(1)}, bf16[1,16,128]{2,1,0:T(8,128)(2,1)S(1)}, u32[]{:S(2)}, u32[]{:S(2)}) collective-permute-start(bf16[1,16,128]{2,1,0:T(8,128)(2,1)S(1)} %get-tuple-element.179), channel_id=1, source_target_pairs={{0,4},{4,8},{8,12},{1,5},{5,9},{9,13},{2,6},{6,10},{10,14},{3,7},{... | collective-permute-start | bytes 12296 | tf_op jit(solution)/shard_map/ppermute | solution.py:31
  107.2 4.4 %collective-permute-start.11 = (bf16[1,16,128]{2,1,0:T(8,128)(2,1)S(1)}, bf16[1,16,128]{2,1,0:T(8,128)(2,1)S(1)}, u32[]{:S(2)}, u32[]{:S(2)}) collective-permute-start(bf16[1,16,128]{2,1,0:T(8,128)(2,1)S(1)} %get-tuple-element.180), channel_id=1, source_target_pairs={{4,0},{8,4},{12,8},{5,1},{9,5},{13,9},{6,2},{10,6},{14,10},{7,3},{... | collective-permute-start | bytes 12296 | tf_op jit(solution)/shard_map/ppermute | solution.py:32
  111.5 5.5 %collective-permute-start.12 = (bf16[18,1,128]{2,1,0:T(2,128)(2,1)S(1)}, bf16[18,1,128]{2,1,0:T(2,128)(2,1)S(1)}, u32[]{:S(2)}, u32[]{:S(2)}) collective-permute-start(bf16[18,1,128]{2,1,0:T(2,128)(2,1)S(1)} %get-tuple-element.167), channel_id=1, source_target_pairs={{0,1},{1,2},{2,3},{4,5},{5,6},{6,7},{8,9},{9,10},{10,11},{12,13},{... | collective-permute-start | bytes 13832 | tf_op jit(solution)/shard_map/ppermute | solution.py:31
  114.9 5.0 %collective-permute-start.13 = (bf16[18,1,128]{2,1,0:T(2,128)(2,1)S(1)}, bf16[18,1,128]{2,1,0:T(2,128)(2,1)S(1)}, u32[]{:S(2)}, u32[]{:S(2)}) collective-permute-start(bf16[18,1,128]{2,1,0:T(2,128)(2,1)S(1)} %get-tuple-element.168), channel_id=1, source_target_pairs={{1,0},{2,1},{3,2},{5,4},{6,5},{7,6},{9,8},{10,9},{11,10},{13,12},{... | collective-permute-start | bytes 13832 | tf_op jit(solution)/shard_map/ppermute | solution.py:32
Sparse Core Ops, SparseCore 0:
  47.3 20.3 reduce-scatter.1
